TPU v7x, 512 devices: a whole 4x8x8 slice. The times are simulated.
512 devices in a mesh: blk: 64 (over y_hi, z, core), head: 8 (over y_lo, x).
Axes of the slice: x: 4, y: 8 (y_hi: 4, y_lo: 2; y = y_hi * 2 + y_lo), z: 8, core: 2. Of those that a mesh axis runs over, the one named last changes fastest.
Arguments:
- queries: bfloat16 [8192, 4096], P(('blk', 'head')), may hold values from -8 to 8
- keys: bfloat16 [8192, 1024], P(('blk', 'head')), may hold values from -8 to 8
- values: bfloat16 [8192, 1024], P(('blk', 'head')), may hold values from -6 to 6
- outputs: bfloat16 [8192, 4096], P(('blk', 'head')), may hold values from -4 to 4
- grad_out: bfloat16 [8192, 4096], P(('blk', 'head')), may hold values from -6 to 6
- span_order: int32 [64], replicated, may hold values from 0 to 63, each once
Outputs:
- grad_queries: bfloat16 [8192, 4096], P(('blk', 'head'))
- grad_keys: bfloat16 [8192, 1024], P(('blk', 'head'))
- grad_values: bfloat16 [8192, 1024], P(('blk', 'head'))
Inputs may be any that keep to these rules, and one draw needn't show every extreme that they name: Block k of 128 stored rows of every token array holds the sequence's span span_order[k]; each span once.
All inputs are finite; a program needn't handle non-finite values.
Results may differ from a plain program's by a relative error of at most 0.0051.
Values may be sent and summed in bfloat16 or wider, within the bound.
A program may use at most 64 MiB of HBM per device.

v0:
```python
import math

import jax
import jax.numpy as jnp
from jax import lax
from jax.sharding import PartitionSpec as P

QHEADS = 32
KVHEADS = 8
HEAD_DIM = 128


NEG = -1e30


def from_behind(array, axis, by):
    peers = lax.axis_size(axis)
    return lax.ppermute(array, axis, [(i, (i + by) % peers) for i in range(peers)])


def on_device(queries, keys, values, outputs, grad_out, span_order):
    cycle_n = lax.axis_size("blk")
    query_h, output_h, grad_h, key_h, value_h = (
        lax.all_to_all(queries, "head", split_axis=1, concat_axis=0, tiled=True),
        lax.all_to_all(outputs, "head", split_axis=1, concat_axis=0, tiled=True),
        lax.all_to_all(grad_out, "head", split_axis=1, concat_axis=0, tiled=True),
        lax.all_to_all(keys, "head", split_axis=1, concat_axis=0, tiled=True),
        lax.all_to_all(values, "head", split_axis=1, concat_axis=0, tiled=True),
    )
    span_rows = query_h.shape[0]
    kv_local = key_h.shape[1] // HEAD_DIM
    group_size = QHEADS // KVHEADS
    inv_root = 1.0 / math.sqrt(HEAD_DIM)
    query_four = query_h.reshape(span_rows, kv_local, group_size, HEAD_DIM)
    output_four = output_h.reshape(span_rows, kv_local, group_size, HEAD_DIM)
    grad_four = grad_h.reshape(span_rows, kv_local, group_size, HEAD_DIM)
    key_three = key_h.reshape(span_rows, kv_local, HEAD_DIM)
    value_three = value_h.reshape(span_rows, kv_local, HEAD_DIM)
    rowdot = jnp.einsum(
        "tkgd,tkgd->kgt", grad_four, output_four, preferred_element_type=jnp.float32
    )
    my_block = lax.axis_index("blk")
    my_pos = span_order[my_block] * span_rows + jnp.arange(span_rows, dtype=jnp.int32)
    directions = (1,)
    row_starts = (0,)

    def source_block(cycle_step, direction):
        return (my_block - direction * cycle_step) % cycle_n

    def key_positions(cycle_step, direction, row_start):
        source = source_block(cycle_step, direction)
        return span_order[source] * span_rows + row_start + jnp.arange(span_rows, dtype=jnp.int32)

    def tile_scores(key_rows, key_pos):
        scores = (
            jnp.einsum("tkgd,ukd->kgtu", query_four, key_rows, preferred_element_type=jnp.float32)
            * inv_root
        )
        allowed = key_pos[None, :] <= my_pos[:, None]
        return (scores, allowed)

    def stats_tile(running, key_rows, key_pos):
        running_max, running_sum = running
        scores, allowed = tile_scores(key_rows, key_pos)
        masked = jnp.where(allowed, scores, NEG)
        new_max = jnp.maximum(running_max, jnp.max(masked, axis=-1))
        weights = jnp.where(allowed, jnp.exp(scores - new_max[..., None]), 0.0)
        return (new_max, running_sum * jnp.exp(running_max - new_max) + jnp.sum(weights, axis=-1))

    def rotate_keys(pieces):
        return (from_behind(pieces[0], "blk", 1),)

    def rotate_pairs(pieces):
        return (from_behind(pieces[0], "blk", 1),)

    def rotate_grads(pieces):
        return (from_behind(pieces[0], "blk", 1),)

    def stats_compute(cycle_step, pieces, softmax_stats):
        key_pos = key_positions(cycle_step, directions[0], row_starts[0])
        softmax_stats = stats_tile(softmax_stats, pieces[0], key_pos)
        return softmax_stats

    def grad_tile(running, pair_rows, key_pos):
        query_acc, carried = running
        scores, allowed = tile_scores(pair_rows[0], key_pos)
        probabilities = jnp.where(allowed, jnp.exp(scores - log_total[..., None]), 0.0)
        dprobs = jnp.einsum(
            "tkgd,ukd->kgtu", grad_four, pair_rows[1], preferred_element_type=jnp.float32
        )
        dscores = (probabilities * (dprobs - rowdot[..., None])).astype(jnp.bfloat16)
        weights_low = probabilities.astype(jnp.bfloat16)
        query_acc = query_acc + jnp.einsum(
            "kgtu,ukd->tkgd", dscores, pair_rows[0], preferred_element_type=jnp.float32
        )
        key_part = jnp.einsum(
            "kgtu,tkgd->ukd", dscores, query_four, preferred_element_type=jnp.float32
        )
        value_part = jnp.einsum(
            "kgtu,tkgd->ukd", weights_low, grad_four, preferred_element_type=jnp.float32
        )
        return (query_acc, carried + jnp.stack([key_part, value_part]))

    def grad_compute(cycle_step, pairs_now, grads_now, query_acc):
        key_pos = key_positions(cycle_step, directions[0], row_starts[0])
        query_acc, carried = grad_tile((query_acc, grads_now[0]), pairs_now[0], key_pos)
        updated = [carried]
        return (tuple(updated), query_acc)

    pair_stack = jnp.stack([key_three, value_three])
    start_stats = (
        jnp.full((kv_local, group_size, span_rows), NEG, jnp.float32),
        jnp.zeros((kv_local, group_size, span_rows), jnp.float32),
    )
    grad_pieces = tuple(
        (jnp.zeros((2, span_rows, kv_local, HEAD_DIM), jnp.float32) for row_start in row_starts)
    )
    query_start = jnp.zeros((span_rows, kv_local, group_size, HEAD_DIM), jnp.float32)

    def stats_turn(cycle_step, state_in):
        pieces, softmax_stats = state_in
        softmax_stats = stats_compute(cycle_step, pieces, softmax_stats)
        return (rotate_keys(pieces), softmax_stats)

    key_pieces = tuple((key_three for row_start in row_starts))
    key_pieces, softmax_stats = lax.fori_loop(0, cycle_n - 1, stats_turn, (key_pieces, start_stats))
    softmax_stats = stats_compute(cycle_n - 1, key_pieces, softmax_stats)
    log_total = softmax_stats[0] + jnp.log(softmax_stats[1])

    def grad_turn(cycle_step, state_in):
        pairs_now, grads_now, query_acc = state_in
        updated, query_acc = grad_compute(cycle_step, pairs_now, grads_now, query_acc)
        return (rotate_pairs(pairs_now), rotate_grads(updated), query_acc)

    pair_pieces = tuple((pair_stack for row_start in row_starts))
    pair_pieces, grad_pieces, query_acc = lax.fori_loop(
        0, cycle_n - 1, grad_turn, (pair_pieces, grad_pieces, query_start)
    )
    grad_pieces, query_acc = grad_compute(cycle_n - 1, pair_pieces, grad_pieces, query_acc)
    grads_home = jnp.concatenate(rotate_grads(grad_pieces), axis=1)
    grad_q = (
        (query_acc * inv_root)
        .astype(jnp.bfloat16)
        .reshape(span_rows, kv_local * group_size * HEAD_DIM)
    )
    grad_k = (grads_home[0] * inv_root).astype(jnp.bfloat16).reshape(span_rows, kv_local * HEAD_DIM)
    grad_v = grads_home[1].astype(jnp.bfloat16).reshape(span_rows, kv_local * HEAD_DIM)
    grad_queries, grad_keys, grad_values = (
        lax.all_to_all(grad_q, "head", split_axis=0, concat_axis=1, tiled=True),
        lax.all_to_all(grad_k, "head", split_axis=0, concat_axis=1, tiled=True),
        lax.all_to_all(grad_v, "head", split_axis=0, concat_axis=1, tiled=True),
    )
    return (grad_queries, grad_keys, grad_values)


def solution(mesh):
    placed = (
        P(("blk", "head"), None),
        P(("blk", "head"), None),
        P(("blk", "head"), None),
        P(("blk", "head"), None),
        P(("blk", "head"), None),
        P(),
    )
    return jax.shard_map(
        on_device,
        mesh=mesh,
        in_specs=placed,
        out_specs=(P(("blk", "head"), None), P(("blk", "head"), None), P(("blk", "head"), None)),
        check_vma=False,
    )
```

profile of v0, /device:TPU:1, one launch (start us, length us, event | category | flops | bytes accessed | tf_op | source)
XLA Modules:
  0.0 1614.2 jit_solution(17838516427462132123)
XLA Ops:
  2.0 5.9 all-to-all-start
  48.4 598.8 %while.40 = (s32[]{:T(128)}, bf16[128,1,128]{2,0,1:T(8,128)(2,1)S(1)}, f32[1,4,128]{2,1,0:T(4,128)S(1)}, f32[1,4,128]{2,1,0:T(4,128)S(1)}, s32[]{:T(128)}, /*ind...) while((s32[]{:T(128)}, ...), condition=%wide.region_3.4_spmd.clone, body=%wide.region_0.3_spmd.clone.sunk | while | flops 17189648 | bytes 962923 | solution.py:126
  48.4 10.4 collective-permute-start
  74.0 5.8 collective-permute-done
  83.4 5.8 collective-permute-done
  92.9 5.8 collective-permute-done
  102.3 5.8 collective-permute-done
  111.8 6.2 collective-permute-done
  121.6 5.8 collective-permute-done
  131.0 5.8 collective-permute-done
  140.5 5.8 collective-permute-done
  149.9 5.8 collective-permute-done
  159.4 5.8 collective-permute-done
  178.2 5.8 collective-permute-done
  187.7 5.8 collective-permute-done
  197.1 5.8 collective-permute-done
  206.6 5.8 collective-permute-done
  234.9 5.8 collective-permute-done
  244.4 5.8 collective-permute-done
  253.8 5.8 collective-permute-done
  263.3 5.8 collective-permute-done
  282.1 5.8 collective-permute-done
  301.0 5.8 collective-permute-done
  310.5 5.8 collective-permute-done
  338.8 5.8 collective-permute-done
  348.3 5.8 collective-permute-done
  357.7 5.8 collective-permute-done
  367.2 6.2 collective-permute-done
  377.0 5.8 collective-permute-done
  386.4 5.8 collective-permute-done
  405.3 5.8 collective-permute-done
  433.6 5.8 collective-permute-done
  443.1 5.8 collective-permute-done
  462.0 5.8 collective-permute-done
  480.9 5.8 collective-permute-done
  490.3 5.8 collective-permute-done
  499.7 5.8 collective-permute-done
  509.2 5.8 collective-permute-done
  537.5 5.8 collective-permute-done
  547.0 5.8 collective-permute-done
  556.4 5.8 collective-permute-done
  565.9 5.8 collective-permute-done
  594.2 5.8 collective-permute-done
  603.7 5.8 collective-permute-done
  613.1 5.8 collective-permute-done
  641.4 5.8 collective-permute-done
  647.6 927.1 %while.41 = (s32[]{:T(128)}, bf16[2,128,1,128]{3,1,2,0:T(8,128)(2,1)S(1)}, f32[2,128,1,128]{3,1,2,0:T(8,128)S(1)}, f32[128,1,4,128]{3,0,2,1:T(8,128)S(1)}, s32[]...) while((s32[]{:T(128)}, ...), condition=%wide.region_7.8_spmd.clone, body=%wide.region_6.7_spmd.clone.sunk | while | flops 84558096 | bytes 3807658 | solution.py:136
  1577.5 8.4 collective-permute-done.3
  (1723 shorter events, 1241.6 us)
Async XLA Ops:
  2.0 11.0 all-to-all-start
  48.4 12.5 collective-permute-start
  665.4 10.6 collective-permute-start.2
  749.1 10.7 collective-permute-start.1
  753.2 10.8 collective-permute-start.2
  764.1 11.0 collective-permute-start.1
  768.1 11.1 collective-permute-start.2
  798.0 10.6 collective-permute-start.2
  812.7 10.6 collective-permute-start.2
  827.4 10.6 collective-permute-start.2
  842.1 10.6 collective-permute-start.2
  856.8 10.6 collective-permute-start.2
  871.5 10.6 collective-permute-start.2
  886.2 10.6 collective-permute-start.2
  900.9 10.6 collective-permute-start.2
  915.6 10.6 collective-permute-start.2
  930.3 10.6 collective-permute-start.2
  945.0 10.6 collective-permute-start.2
  959.7 10.6 collective-permute-start.2
  974.4 10.6 collective-permute-start.2
  989.1 10.6 collective-permute-start.2
  1033.3 10.6 collective-permute-start.2
  1048.0 10.6 collective-permute-start.2
  1062.7 10.6 collective-permute-start.2
  1077.4 10.6 collective-permute-start.2
  1092.1 10.6 collective-permute-start.2
  1136.2 10.6 collective-permute-start.2
  1150.9 10.6 collective-permute-start.2
  1180.3 10.6 collective-permute-start.2
  1195.0 10.6 collective-permute-start.2
  1209.7 10.6 collective-permute-start.2
  1224.4 10.6 collective-permute-start.2
  1239.1 10.6 collective-permute-start.2
  1253.8 10.6 collective-permute-start.2
  1283.2 10.6 collective-permute-start.2
  1298.0 10.6 collective-permute-start.2
  1342.1 10.6 collective-permute-start.2
  1356.8 10.6 collective-permute-start.2
  1371.5 10.6 collective-permute-start.2
  1386.2 10.6 collective-permute-start.2
  1400.9 10.6 collective-permute-start.2
  1445.0 10.6 collective-permute-start.2
  1459.7 10.6 collective-permute-start.2
  1489.1 10.6 collective-permute-start.2
  1503.8 10.6 collective-permute-start.2
  1533.2 10.6 collective-permute-start.2
  1543.9 11.9 collective-permute-start.1
  1547.9 12.0 collective-permute-start.2
  (155 other events, 1524.4 us)
where the time goes:
time: 1630 us; the launch traced here: 1610 us
  waiting for transfers between devices  933 us (57%)
  starting transfers between devices  404 us (25%)
  loops' own time  94.7 us (6%)
  local copies, waits for them, and re-layouts  84.4 us (5%)
  matrix products  76.3 us (5%)
  other arithmetic  19.5 us (1%)
    ppermute x190, waiting for transfers between devices, from_behind(): lax.ppermute(array, axis, [(i, (i + by) % peers) for i in range(peers)])  900 us
    ppermute x190, starting transfers between devices, from_behind(): lax.ppermute(array, axis, [(i, (i + by) % peers) for i in range(peers)])  373 us
    dynamic_slice x127, local copies, waits for them, and re-layouts, key_positions(): span_order[source] * span_rows + row_start  74.5 us
    another operation x1, loops' own time, on_device(): lax.fori_loop(0, cycle_n - 1, grad_turn, (pair_pieces, grad_pieces, query...  48.4 us
    another operation x1, loops' own time, on_device(): lax.fori_loop(0, cycle_n - 1, stats_turn, (key_pieces, start_stats))  46.3 us
  transfers between devices with their start and end apart: 198, of which 198 were waited for; matrix products, arithmetic and copies ran while one was open for 11% of the time, Pallas kernels for 0%

commit v1 on v0

v1 whole, which is shorter than its diff:
```python
import math

import jax
import jax.numpy as jnp
from jax import lax
from jax.experimental import pallas as pl
from jax.experimental.pallas import tpu as pltpu
from jax.sharding import PartitionSpec as P

NX, NY, NZ, NC = 4, 8, 8, 2
ROWS = 16
HD = 128
GROUP = 4
W = GROUP * HD
NEG = -1e30
MESH = pl.DeviceIdType.MESH
F32 = jnp.float32
BF16 = jnp.bfloat16
INV_ROOT = 1.0 / math.sqrt(HD)
LOG2E = 1.4426950408889634


def near_first(n):
    order = [0]
    for step in range(1, n):
        if step not in order:
            order.append(step)
        if n - step not in order and n - step > 0:
            order.append(n - step)
    return order


def dot_nt(a, b):
    return lax.dot_general(a, b, (((1,), (1,)), ((), ())), preferred_element_type=F32)


def dot_nn(a, b):
    return lax.dot_general(a, b, (((1,), (0,)), ((), ())), preferred_element_type=F32)


def dot_tn(a, b):
    return lax.dot_general(a, b, (((0,), (0,)), ((), ())), preferred_element_type=F32)


def kernel(
    q_in, k_in, v_in, o_in, g_in, order,
    q_out, k_out, v_out,
    o_buf, g_buf, r_buf, qd, kv, pos_u, pos_t, e_buf, dp_buf, m_buf, st, lse,
    dq_acc, dq_send, dq_recv, sib_send, sib_recv, y_send, y_recv, own_dkv, dq_fin, dkv_fin,
    loc_sem, a_send, a_recv, x_send, x_recv, f_send, f_recv, kvr_send, kvr_recv, kvl_send, kvl_recv,
    ks_send, ks_recv, st_send, st_recv, sb_send, sb_recv, yd_send, yd_recv, xd_send, xd_recv, zo_send, zo_recv,
):
    T = NZ * ROWS
    NJ = NC * NY // 2
    NP = NY // 2
    blk = lax.axis_index("blk")
    sub = lax.axis_index("head")
    core = blk % NC
    z = (blk // NC) % NZ
    yh = blk // (NC * NZ)
    x = sub % NX
    yl = sub // NX
    y = yh * 2 + yl
    slot = core * NY + y

    def dev(xx, yy, zz, cc):
        return ((yy // 2) * (NZ * NC) + zz * NC + cc, (yy % 2) * NX + xx)

    def at_x(d):
        return dev((x + d) % NX, y, z, core)

    def at_y(d):
        return dev(x, (y + d) % NY, z, core)

    def at_z(d):
        return dev(x, y, (z + d) % NZ, core)

    sibling = dev(x, y, z, (core + 1) % NC)

    def remote(src, dst, send_sem, recv_sem, who):
        return pltpu.make_async_remote_copy(
            src_ref=src, dst_ref=dst, send_sem=send_sem, recv_sem=recv_sem, device_id=who, device_id_type=MESH
        )

    def zrow(index):
        return pl.ds(pl.multiple_of(index * ROWS, ROWS), ROWS)

    def zcol(index, width):
        return pl.ds(pl.multiple_of(index * width, width), width)

    local = [
        pltpu.make_async_copy(o_in, o_buf, loc_sem.at[0]),
        pltpu.make_async_copy(g_in, g_buf, loc_sem.at[1]),
        pltpu.make_async_copy(k_in.at[:, zcol(z, HD)], kv.at[0, slot, zrow(z), :], loc_sem.at[2]),
        pltpu.make_async_copy(v_in.at[:, zcol(z, HD)], kv.at[1, slot, zrow(z), :], loc_sem.at[3]),
        pltpu.make_async_copy(q_in.at[:, zcol(z, W)], qd.at[x, zrow(z), pl.ds(0, W)], loc_sem.at[4]),
        pltpu.make_async_copy(g_in.at[:, zcol(z, W)], qd.at[x, zrow(z), pl.ds(W, W)], loc_sem.at[5]),
    ]
    for copy in local:
        copy.start()

    barrier = pltpu.get_barrier_semaphore()
    peers = [at_z(d) for d in range(1, NZ)] + [at_x(d) for d in range(1, NX)] + [at_y(d) for d in range(1, NY)]
    if NC == 2:
        peers.append(sibling)
    for who in peers:
        pl.semaphore_signal(barrier, inc=1, device_id=who, device_id_type=MESH)
    pl.semaphore_wait(barrier, len(peers))

    z_order = near_first(NZ)

    def a_copy(kind, d):
        to = (z + d) % NZ
        src, dst = {
            0: (k_in.at[:, zcol(to, HD)], kv.at[0, slot, zrow(z), :]),
            1: (v_in.at[:, zcol(to, HD)], kv.at[1, slot, zrow(z), :]),
            2: (q_in.at[:, zcol(to, W)], qd.at[x, zrow(z), pl.ds(0, W)]),
            3: (g_in.at[:, zcol(to, W)], qd.at[x, zrow(z), pl.ds(W, W)]),
            4: (r_buf.at[to], qd.at[x, zrow(z), pl.ds(2 * W, HD)]),
        }[kind]
        return remote(src, dst, a_send.at[kind, d], a_recv.at[kind, d], at_z(d))

    def a_arrived(kind, d):
        row = zrow((z + NZ - d) % NZ)
        ref = {
            0: kv.at[0, slot, row, :],
            1: kv.at[1, slot, row, :],
            2: qd.at[x, row, pl.ds(0, W)],
            3: qd.at[x, row, pl.ds(W, W)],
            4: qd.at[x, row, pl.ds(2 * W, HD)],
        }[kind]
        remote(ref, ref, a_send.at[kind, d], a_recv.at[kind, d], at_z(d)).wait_recv()

    for d in z_order[1:]:
        a_copy(0, d).start()
        a_copy(1, d).start()
    for d in z_order[1:]:
        a_copy(2, d).start()
        a_copy(3, d).start()

    local[0].wait()
    local[1].wait()
    lane = lax.broadcasted_iota(jnp.int32, (ROWS, HD), 1)

    def rowdots(zz, carry):
        spread = jnp.zeros((ROWS, HD), F32)
        for h in range(GROUP):
            cols = pl.ds(pl.multiple_of(zz * W + h * HD, HD), HD)
            dots = jnp.sum(g_buf[:, cols].astype(F32) * o_buf[:, cols].astype(F32), axis=1, keepdims=True)
            spread = jnp.where(lane // 32 == h, dots, spread)
        high = spread.astype(BF16).astype(F32)
        rest = spread - high
        middle = rest.astype(BF16).astype(F32)
        low = rest - middle
        piece = lane % 32
        pieces = jnp.where(piece == 0, high, jnp.where(piece == 1, middle, jnp.where(piece == 2, low, 0.0)))
        r_buf[zz] = pieces.astype(BF16)
        return carry

    lax.fori_loop(0, NZ, rowdots, 0)
    for d in z_order[1:]:
        a_copy(4, d).start()
    qd[x, zrow(z), pl.ds(2 * W, HD)] = r_buf[z]

    row_in = lax.broadcasted_iota(jnp.int32, (ROWS, HD), 0)
    for cc in range(NC):
        for yy in range(NY):
            for zz in range(NZ):
                base = order[(yy // 2) * (NZ * NC) + zz * NC + cc] * 128 + ((yy % 2) * NX + x) * ROWS
                pos_u[cc * NY + yy, pl.ds(zz * ROWS, ROWS), :] = row_in + base
    t_lane = lax.broadcasted_iota(jnp.int32, (8, T), 1)
    row_pos = jnp.zeros((8, T), jnp.int32)
    for zz in range(NZ):
        base = order[yh * (NZ * NC) + zz * NC + core] * 128 + yl * NX * ROWS
        row_pos = jnp.where(t_lane // ROWS == zz, base + t_lane % ROWS, row_pos)
    pos_t[...] = row_pos

    n_right, n_left = NY // 2, NY - 1 - NY // 2

    def kv_block(d):
        ref = kv.at[:, core * NY + (y + d + NY) % NY]
        return ref

    def right_copy(s):
        ref = kv_block(-s)
        return remote(ref, ref, kvr_send.at[s], kvr_recv.at[s], at_y(1))

    def left_copy(s):
        ref = kv_block(s)
        return remote(ref, ref, kvl_send.at[s], kvl_recv.at[s], at_y(NY - 1))

    def core_copy(d):
        ref = kv_block(d)
        return remote(ref, ref, ks_send.at[d % NY], ks_recv.at[d % NY], sibling)

    def kv_step(s):
        if s > 0:
            if s <= n_right:
                ref = kv_block(-s)
                remote(ref, ref, kvr_send.at[s - 1], kvr_recv.at[s - 1], at_y(1)).wait_recv()
            if s <= n_left:
                ref = kv_block(s)
                remote(ref, ref, kvl_send.at[s - 1], kvl_recv.at[s - 1], at_y(NY - 1)).wait_recv()
        if s < n_right:
            right_copy(s).start()
        if s < n_left:
            left_copy(s).start()
        if NC == 2:
            if s <= n_right:
                core_copy(-s).start()
            if 0 < s <= n_left:
                core_copy(s).start()

    local[2].wait()
    local[3].wait()
    for d in z_order[1:]:
        a_arrived(0, d)
        a_arrived(1, d)
    kv_step(0)

    half = (NZ + 1) // 2

    def x_piece(dx, d):
        return qd.at[(x + dx + NX) % NX, zrow((z + NZ - d) % NZ), :]

    def x_copy(way, d):
        ref = x_piece(0, d)
        return remote(ref, ref, x_send.at[way, d], x_recv.at[way, d], at_x(1 if way == 0 else NX - 1))

    def x_arrived(way, d):
        ref = x_piece(-1 if way == 0 else 1, d)
        remote(ref, ref, x_send.at[way, d], x_recv.at[way, d], at_x(1)).wait_recv()

    def far_copy(d):
        way = 0 if d < half else 1
        ref = x_piece(-1 if way == 0 else 1, d)
        return remote(ref, ref, f_send.at[d], f_recv.at[d], at_x(1 if way == 0 else NX - 1))

    def far_arrived(d):
        ref = x_piece(2, d)
        remote(ref, ref, f_send.at[d], f_recv.at[d], at_x(1)).wait_recv()

    def forward(d):
        x_arrived(0, d)
        x_arrived(1, d)
        far_copy(d).start()

    local[4].wait()
    local[5].wait()
    kv_steps = list(range(1, max(n_right, n_left) + 1))
    for i, d in enumerate(z_order):
        if d > 0:
            for kind in (2, 3, 4):
                a_arrived(kind, d)
        x_copy(0, d).start()
        x_copy(1, d).start()
        if i >= 2:
            forward(z_order[i - 2])
        if i % 2 == 1 and kv_steps:
            kv_step(kv_steps.pop(0))
    for s in kv_steps:
        kv_step(s)
    for d in z_order[max(0, NZ - 2):]:
        forward(d)
    if NC == 2:
        for d in range(NY):
            ref = kv.at[:, ((core + 1) % NC) * NY + (y + d) % NY]
            remote(ref, ref, ks_send.at[d], ks_recv.at[d], sibling).wait_recv()

    scale = INV_ROOT * LOG2E

    def stack_heads(ref, xs, first):
        return jnp.concatenate([ref[xs, :, first + h * HD:first + (h + 1) * HD] for h in range(GROUP)], axis=0)

    def key_rows(which, j):
        return kv[which, pl.ds(2 * j, 2)].reshape(2 * T, HD)

    def score_part(xs):
        queries = stack_heads(qd, xs, 0)
        t_pos = pos_t[0:1, :] + xs * ROWS

        def body(j, running):
            run_max, run_sum = running
            s = dot_nt(key_rows(0, j), queries)
            seen = pos_u[pl.ds(2 * j, 2)].reshape(2 * T, HD)[:, :T] <= t_pos
            tops, sums = [], []
            for h in range(GROUP):
                part = jnp.where(seen, s[:, h * T:(h + 1) * T] * scale, NEG)
                top = jnp.max(part, axis=0, keepdims=True)
                e = jnp.exp2(part - top)
                e_buf[j, xs, :, h * T:(h + 1) * T] = e
                tops.append(top)
                sums.append(jnp.sum(e, axis=0, keepdims=True))
            top = jnp.concatenate(tops, axis=1)
            total = jnp.concatenate(sums, axis=1)
            m_buf[j, xs] = top
            new_max = jnp.maximum(run_max, top)
            new_sum = run_sum * jnp.exp2(run_max - new_max) + total * jnp.exp2(top - new_max)
            return new_max, new_sum

        start = (jnp.full((1, GROUP * T), NEG, F32), jnp.zeros((1, GROUP * T), F32))
        run_max, run_sum = lax.fori_loop(0, NJ, body, start)
        st[x, xs, 0:1, :] = run_max
        st[x, xs, 1:2, :] = run_sum

    pick_row = lax.broadcasted_iota(jnp.int32, (8, HD), 0)
    pick_lane = lax.broadcasted_iota(jnp.int32, (8, HD), 1)
    pick = jnp.where((pick_lane // 32 == pick_row) & (pick_lane % 32 < 3), 1.0, 0.0).astype(BF16)

    def dprobs_part(xs):
        cotangents = stack_heads(qd, xs, W)
        rowdot = dot_nt(pick, qd[xs, :, 2 * W:])
        rowdot = jnp.concatenate([rowdot[h:h + 1, :] for h in range(GROUP)], axis=1)

        def body(j, carry):
            dp_buf[j, xs] = dot_nt(key_rows(1, j), cotangents) - rowdot
            return carry

        lax.fori_loop(0, NJ, body, 0)

    for dx in (0, NX - 1, 1):
        score_part((x + dx) % NX)
        dprobs_part((x + dx) % NX)
    for d in z_order:
        far_arrived(d)
    score_part((x + 2) % NX)

    def st_copy(d):
        return remote(st.at[x], st.at[x], st_send.at[d], st_recv.at[d], at_x(d))

    for d in range(1, NX):
        st_copy(d).start()
    dprobs_part((x + 2) % NX)
    for d in range(1, NX):
        ref = st.at[(x + NX - d) % NX]
        remote(ref, ref, st_send.at[d], st_recv.at[d], at_x(d)).wait_recv()
    for xs in range(NX):
        top = st[0, xs, 0:1, :]
        for other in range(1, NX):
            top = jnp.maximum(top, st[other, xs, 0:1, :])
        total = jnp.zeros((1, GROUP * T), F32)
        for other in range(NX):
            total = total + st[other, xs, 1:2, :] * jnp.exp2(st[other, xs, 0:1, :] - top)
        lse[xs] = top + jnp.log2(total)
    dq_acc[...] = jnp.zeros_like(dq_acc)

    def grad_chunk(j):
        keys = key_rows(0, j)
        dk = jnp.zeros((2 * T, HD), F32)
        dv = jnp.zeros((2 * T, HD), F32)
        for xs in range(NX):
            p = e_buf[j, xs] * jnp.exp2(m_buf[j, xs] - lse[xs])
            ds = (p * dp_buf[j, xs]).astype(BF16)
            dk = dk + dot_nn(ds, stack_heads(qd, xs, 0))
            dv = dv + dot_nn(p.astype(BF16), stack_heads(qd, xs, W))
            dq_acc[xs] += dot_tn(keys, ds)
        return dk, dv

    def sib_copy(p):
        return remote(sib_send.at[p], sib_recv.at[p], sb_send.at[p], sb_recv.at[p], sibling)

    if NC == 2:

        def other_core(p, carry):
            dk, dv = grad_chunk(((core + 1) % NC) * NP + p)
            sib_send[p, 0] = dk.astype(BF16)
            sib_send[p, 1] = dv.astype(BF16)
            sib_copy(p).start()
            return carry

        lax.fori_loop(0, NP, other_core, 0)

    def y_copy(p, half_of):
        d = (2 * p + half_of - y + 2 * NY) % NY
        src = y_send.at[p, :, pl.ds(pl.multiple_of(half_of * T, T), T), :]
        return remote(src, y_recv.at[d], yd_send.at[d], yd_recv.at[d], at_y(d))

    def own_core(p):
        dk, dv = grad_chunk(core * NP + p)
        if NC == 2:
            sib_copy(p).wait_recv()
            dk = dk + sib_recv[p, 0].astype(F32)
            dv = dv + sib_recv[p, 1].astype(F32)
        y_send[p, 0] = dk.astype(BF16)
        y_send[p, 1] = dv.astype(BF16)
        return dk, dv

    far_pairs = [NP // 2] + [d for d in range(1, NP) if d != NP // 2] if NP > 1 else []

    def far_pair(i, carry):
        p = (yh + (NP // 2 + i) % (NP - 1) + 1) % NP if NP > 2 else (yh + 1) % NP
        own_core(p)
        y_copy(p, 0).start()
        y_copy(p, 1).start()
        return carry

    if far_pairs:
        lax.fori_loop(0, NP - 1, far_pair, 0)
    dk, dv = own_core(yh)
    own_dkv[0] = dk
    own_dkv[1] = dv
    y_copy(yh, 1 - yl).start()

    def dq_copy(d):
        to = (x + d) % NX
        return remote(dq_send.at[to], dq_recv.at[d], xd_send.at[d], xd_recv.at[d], at_x(d))

    dq_send[...] = dq_acc[...].astype(BF16)
    for d in (2, 1, 3):
        dq_copy(d).start()

    def out_copy(kind, d):
        to = (z + d) % NZ
        src, dst = {
            0: (dq_fin.at[zrow(to), :], q_out.at[:, zcol(z, W)]),
            1: (dkv_fin.at[0, zrow(to), :], k_out.at[:, zcol(z, HD)]),
            2: (dkv_fin.at[1, zrow(to), :], v_out.at[:, zcol(z, HD)]),
        }[kind]
        if d == 0:
            return pltpu.make_async_copy(src, dst, zo_send.at[kind, 0])
        return remote(src, dst, zo_send.at[kind, d], zo_recv.at[kind, d], at_z(d))

    own_rows = pl.ds(pl.multiple_of(yl * T, T), T)
    sums = [own_dkv[0, own_rows, :], own_dkv[1, own_rows, :]]
    for d in range(1, NY):
        ref = y_recv.at[d]
        remote(ref, ref, yd_send.at[d], yd_recv.at[d], at_y(d)).wait_recv()
        sums = [sums[i] + y_recv[d, i].astype(F32) for i in range(2)]
    dkv_fin[0] = (sums[0] * INV_ROOT).astype(BF16)
    dkv_fin[1] = sums[1].astype(BF16)
    for d in z_order:
        out_copy(1, d).start()
        out_copy(2, d).start()

    dq = dq_acc[x]
    for d in range(1, NX):
        ref = dq_recv.at[d]
        remote(ref, ref, xd_send.at[d], xd_recv.at[d], at_x(d)).wait_recv()
        dq = dq + dq_recv[d].astype(F32)
    dq = dq * INV_ROOT
    for h in range(GROUP):
        dq_fin[:, h * HD:(h + 1) * HD] = dq[:, h * T:(h + 1) * T].T.astype(BF16)
    for d in z_order:
        out_copy(0, d).start()

    for kind in range(3):
        out_copy(kind, 0).wait()
    for d in z_order[1:]:
        src = (z + NZ - d) % NZ
        for kind, ref in (
            (0, q_out.at[:, zcol(src, W)]),
            (1, k_out.at[:, zcol(src, HD)]),
            (2, v_out.at[:, zcol(src, HD)]),
        ):
            remote(ref, ref, zo_send.at[kind, d], zo_recv.at[kind, d], at_z(d)).wait_recv()
    for d in z_order[1:]:
        for kind in range(5):
            a_copy(kind, d).wait_send()
        for kind in range(3):
            out_copy(kind, d).wait_send()
    for d in range(NZ):
        x_copy(0, d).wait_send()
        x_copy(1, d).wait_send()
        far_copy(d).wait_send()
    for s in range(n_right):
        right_copy(s).wait_send()
    for s in range(n_left):
        left_copy(s).wait_send()
    if NC == 2:
        for d in range(NY):
            core_copy(d).wait_send()
        for p in range(NP):
            sib_copy(p).wait_send()
    for d in range(1, NX):
        st_copy(d).wait_send()
        dq_copy(d).wait_send()
    for d in range(1, NY):
        ref = y_recv.at[d]
        remote(ref, ref, yd_send.at[d], yd_recv.at[d], at_y(d)).wait_send()


def on_device(queries, keys, values, outputs, grad_out, span_order):
    T = NZ * ROWS
    NJ = NC * NY // 2
    NP = NY // 2
    QW = 2 * W + HD
    vmem = pltpu.VMEM
    dma = pltpu.SemaphoreType.DMA
    width = W * NZ
    kv_width = HD * NZ
    scratch = [
        vmem((ROWS, width), BF16),
        vmem((ROWS, width), BF16),
        vmem((NZ, ROWS, HD), BF16),
        vmem((NX, T, QW), BF16),
        vmem((2, NC * NY, T, HD), BF16),
        vmem((NC * NY, T, HD), jnp.int32),
        vmem((8, T), jnp.int32),
        vmem((NJ, NX, 2 * T, GROUP * T), F32),
        vmem((NJ, NX, 2 * T, GROUP * T), F32),
        vmem((NJ, NX, 1, GROUP * T), F32),
        vmem((NX, NX, 2, GROUP * T), F32),
        vmem((NX, 1, GROUP * T), F32),
        vmem((NX, HD, GROUP * T), F32),
        vmem((NX, HD, GROUP * T), BF16),
        vmem((NX, HD, GROUP * T), BF16),
        vmem((NP, 2, 2 * T, HD), BF16),
        vmem((NP, 2, 2 * T, HD), BF16),
        vmem((NP, 2, 2 * T, HD), BF16),
        vmem((NY, 2, T, HD), BF16),
        vmem((2, 2 * T, HD), F32),
        vmem((T, W), BF16),
        vmem((2, T, HD), BF16),
        dma((6,)),
        dma((5, NZ)), dma((5, NZ)),
        dma((2, NZ)), dma((2, NZ)),
        dma((NZ,)), dma((NZ,)),
        dma((NY,)), dma((NY,)),
        dma((NY,)), dma((NY,)),
        dma((NY,)), dma((NY,)),
        dma((NX,)), dma((NX,)),
        dma((NP,)), dma((NP,)),
        dma((NY,)), dma((NY,)),
        dma((NX,)), dma((NX,)),
        dma((3, NZ)), dma((3, NZ)),
    ]
    anywhere = pl.BlockSpec(memory_space=pl.ANY)
    return pl.pallas_call(
        kernel,
        out_shape=(
            jax.ShapeDtypeStruct((ROWS, width), BF16),
            jax.ShapeDtypeStruct((ROWS, kv_width), BF16),
            jax.ShapeDtypeStruct((ROWS, kv_width), BF16),
        ),
        in_specs=[anywhere] * 5 + [pl.BlockSpec(memory_space=pltpu.SMEM)],
        out_specs=(anywhere, anywhere, anywhere),
        scratch_shapes=scratch,
        compiler_params=pltpu.CompilerParams(
            collective_id=0, has_side_effects=True, vmem_limit_bytes=60 * 1024 * 1024
        ),
    )(queries, keys, values, outputs, grad_out, span_order)


def solution(mesh):
    rows = P(("blk", "head"), None)
    return jax.shard_map(
        on_device,
        mesh=mesh,
        in_specs=(rows, rows, rows, rows, rows, P()),
        out_specs=(rows, rows, rows),
        check_vma=False,
    )
```

time: 1630 us -> 91.2 us (0.06)
  waiting for transfers between devices: 933 us -> 0 us
  starting transfers between devices: 404 us -> 0 us
  loops' own time: 94.7 us -> 0 us
  Pallas kernels: 0 us -> 87.4 us
  local copies, waits for them, and re-layouts: 84.4 us -> 2.96 us
  matrix products: 76.3 us -> 0 us
  other arithmetic: 19.5 us -> 0 us
    ppermute x190 -> x0, waiting for transfers between devices: 900 us -> none  [from_behind(): lax.ppermute(array, axis, [(i, (i + by) % peers) for i in range(peers)])]
    ppermute x190 -> x0, starting transfers between devices: 373 us -> none  [from_behind(): lax.ppermute(array, axis, [(i, (i + by) % peers) for i in range(peers)])]
    another operation x2 -> x0, loops' own time: 94.7 us -> none  [the longest x1 48.4 us: on_device(): lax.fori_loop(0, cycle_n - 1, grad_turn, (pair_pieces, grad_pieces, query...]
    pallas_call x0 -> x1, Pallas kernels: none -> 87.4 us  [on_device(): pl.pallas_call(kernel, out_shape=(jax.ShapeDtypeStruct((ROWS, width), BF1...]
    dot_general x384 -> x0, matrix products: 76.3 us -> none  [the longest x128 26.5 us: tile_scores(): jnp.einsum('tkgd,ukd->kgtu', query_four, key_rows, preferred_element_type...]
    dynamic_slice x127 -> x0, local copies, waits for them, and re-layouts: 74.5 us -> none  [key_positions(): span_order[source] * span_rows + row_start]
    all_to_all x8 -> x0, waiting for transfers between devices: 32.9 us -> none  [the longest x1 5.23 us: on_device(): lax.all_to_all(outputs, 'head', split_axis=1, concat_axis=0, tiled=True)]
    all_to_all x8 -> x0, starting transfers between devices: 30.9 us -> none  [the longest x1 5.86 us: on_device(): lax.all_to_all(keys, 'head', split_axis=1, concat_axis=0, tiled=True)]
  transfers between devices with their start and end apart: 198 -> 0, of which waited for: 198 -> 0; matrix products, arithmetic and copies ran while one was open for 11% -> 0% of each run, Pallas kernels for 0% -> 0%
where the time goes in v1:
time: 91.2 us; the launch traced here: 91 us
  Pallas kernels  87.4 us (96%)
  local copies, waits for them, and re-layouts  2.96 us (3%)
    pallas_call x1, Pallas kernels, on_device(): pl.pallas_call(kernel, out_shape=(jax.ShapeDtypeStruct((ROWS, width), BF1...  87.4 us
    unnamed x7, local copies, waits for them, and re-layouts  2.96 us

profile of v1, /device:TPU:1, one launch (start us, length us, event | category | flops | bytes accessed | tf_op | source)
XLA Modules:
  0.0 91.0 jit_solution(3805925988860828876)
XLA Ops:
  0.6 87.4 %shard_map.85 = (bf16[16,4096]{1,0:T(8,128)(2,1)}, bf16[16,1024]{1,0:T(8,128)(2,1)}, bf16[16,1024]{1,0:T(8,128)(2,1)}) custom-call(bf16[16,4096]{1,0:T(8,128)(2,1)} %q_in.1, bf16[16,1024]{1,0:T(8,128)(2,1)} %k_in.1, bf16[16,1024]{1,0:T(8,128)(2,1)} %v_in.1, bf16[16,4096]{1,0:T(8,128)(2,1)} %o_in.1, bf16[16,4096]{1,0:T(8,128)(2,1)} %g_in.1, s32[64]{0:T(128)} %order.1), custom_call_target="tpu_custom_call" | custom-call | tf_op jit(solution)/shard_map/pallas_call | solution.py:528
  88.0 0.0 copy-start.1
  88.0 1.6 %copy.12 = bf16[16,4096]{1,0:T(8,128)(2,1)} copy(bf16[16,4096]{1,0:T(8,128)(2,1)} %get-tuple-element.6) | data formatting | bytes 262144
  89.6 0.0 copy-done.1
  89.6 0.0 copy-start
  89.6 0.6 copy.13
  90.2 0.2 copy-done
  90.4 0.6 copy.14
Async XLA Ops:
  88.0 1.6 %copy-start.1 = (bf16[16,1024]{1,0:T(8,128)(2,1)S(1)}, bf16[16,1024]{1,0:T(8,128)(2,1)}, u32[]{:S(2)}) copy-start(bf16[16,1024]{1,0:T(8,128)(2,1)} %get-tuple-element.7) | copy-start | bytes 98308
  89.6 0.8 copy-start

commit v2 on v1

v2 whole, which is shorter than its diff:
```python
import math

import jax
import jax.numpy as jnp
from jax import lax
from jax.experimental import pallas as pl
from jax.experimental.pallas import tpu as pltpu
from jax.sharding import PartitionSpec as P

NX, NY, NZ, NC = 4, 8, 8, 2
ROWS = 16
HD = 128
GROUP = 4
W = GROUP * HD
NEG = -1e30
MESH = pl.DeviceIdType.MESH
F32 = jnp.float32
BF16 = jnp.bfloat16
INV_ROOT = 1.0 / math.sqrt(HD)
LOG2E = 1.4426950408889634


def near_first(n):
    order = [0]
    for step in range(1, n):
        if step not in order:
            order.append(step)
        if n - step not in order and n - step > 0:
            order.append(n - step)
    return order


def dot_nt(a, b):
    return lax.dot_general(a, b, (((1,), (1,)), ((), ())), preferred_element_type=F32)


def dot_nn(a, b):
    return lax.dot_general(a, b, (((1,), (0,)), ((), ())), preferred_element_type=F32)


def dot_tn(a, b):
    return lax.dot_general(a, b, (((0,), (0,)), ((), ())), preferred_element_type=F32)


def kernel(
    q_in, k_in, v_in, o_in, g_in, order,
    q_out, k_out, v_out,
    o_buf, g_buf, r_buf, r_own, rd_buf, qg, kv, pos_u, pos_t, qt_buf, gt_buf, kt_buf, e_buf, dp_buf, ds_buf, m_buf, l_buf, st, lse,
    dq_own, dq_send, dq_recv, sib_send, sib_recv, y_send, y_recv, own_dkv, dq_fin, dkv_fin,
    loc_sem, a_send, a_recv, x_send, x_recv, rd_send, rd_recv, kv_send, kv_recv,
    ks_send, ks_recv, st_send, st_recv, sb_send, sb_recv, yd_send, yd_recv, xd_send, xd_recv, zo_send, zo_recv,
):
    T = NZ * ROWS
    NJ = NC * NY // 2
    NP = NY // 2
    blk = lax.axis_index("blk")
    sub = lax.axis_index("head")
    core = blk % NC
    z = (blk // NC) % NZ
    yh = blk // (NC * NZ)
    x = sub % NX
    yl = sub // NX
    y = yh * 2 + yl
    slot = core * NY + y

    def dev(xx, yy, zz, cc):
        return ((yy // 2) * (NZ * NC) + zz * NC + cc, (yy % 2) * NX + xx)

    def at_x(d):
        return dev((x + d) % NX, y, z, core)

    def at_y(d):
        return dev(x, (y + d) % NY, z, core)

    def at_z(d):
        return dev(x, y, (z + d) % NZ, core)

    sibling = dev(x, y, z, (core + 1) % NC)

    def remote(src, dst, send_sem, recv_sem, who):
        return pltpu.make_async_remote_copy(
            src_ref=src, dst_ref=dst, send_sem=send_sem, recv_sem=recv_sem, device_id=who, device_id_type=MESH
        )

    def zrow(index):
        return pl.ds(pl.multiple_of(index * ROWS, ROWS), ROWS)

    def zcol(index, width):
        return pl.ds(pl.multiple_of(index * width, width), width)

    barrier = pltpu.get_barrier_semaphore()
    peers = [at_z(d) for d in near_first(NZ)[:0:-1]] + [at_y(d) for d in near_first(NY)[:0:-1]]
    peers += [at_x(d) for d in range(1, NX)]
    if NC == 2:
        peers.append(sibling)
    for who in peers:
        pl.semaphore_signal(barrier, inc=1, device_id=who, device_id_type=MESH)

    local = [
        pltpu.make_async_copy(o_in, o_buf, loc_sem.at[0]),
        pltpu.make_async_copy(g_in, g_buf, loc_sem.at[1]),
        pltpu.make_async_copy(q_in.at[:, zcol(z, W)], qg.at[0, x, zrow(z), :], loc_sem.at[2]),
        pltpu.make_async_copy(g_in.at[:, zcol(z, W)], qg.at[1, x, zrow(z), :], loc_sem.at[3]),
        pltpu.make_async_copy(k_in.at[:, zcol(z, HD)], kv.at[0, slot, zrow(z), :], loc_sem.at[4]),
        pltpu.make_async_copy(v_in.at[:, zcol(z, HD)], kv.at[1, slot, zrow(z), :], loc_sem.at[5]),
    ]
    for copy in local:
        copy.start()

    pl.semaphore_wait(barrier, len(peers))

    z_order = near_first(NZ)
    y_order = near_first(NY)

    def a_copy(kind, d):
        to = (z + d) % NZ
        src, dst = {
            0: (k_in.at[:, zcol(to, HD)], kv.at[0, slot, zrow(z), :]),
            1: (v_in.at[:, zcol(to, HD)], kv.at[1, slot, zrow(z), :]),
            2: (q_in.at[:, zcol(to, W)], qg.at[0, x, zrow(z), :]),
            3: (g_in.at[:, zcol(to, W)], qg.at[1, x, zrow(z), :]),
            4: (r_buf.at[to], r_own.at[zrow(z), :]),
        }[kind]
        return remote(src, dst, a_send.at[kind, d], a_recv.at[kind, d], at_z(d))

    def a_arrived(kind, d):
        row = zrow((z + NZ - d) % NZ)
        ref = {
            0: kv.at[0, slot, row, :],
            1: kv.at[1, slot, row, :],
            2: qg.at[0, x, row, :],
            3: qg.at[1, x, row, :],
            4: r_own.at[row, :],
        }[kind]
        remote(ref, ref, a_send.at[kind, d], a_recv.at[kind, d], at_z(d)).wait_recv()

    def x_copy(kind, dx, d):
        ref = qg.at[kind, x, zrow((z + NZ - d) % NZ), :]
        return remote(ref, ref, x_send.at[kind, dx, d], x_recv.at[kind, dx, d], at_x(dx))

    def x_arrived(kind, dx, d):
        ref = qg.at[kind, (x + NX - dx) % NX, zrow((z + NZ - d) % NZ), :]
        remote(ref, ref, x_send.at[kind, dx, d], x_recv.at[kind, dx, d], at_x(dx)).wait_recv()

    def x_piece(kind, d):
        if d > 0:
            a_arrived(2 + kind, d)
        for dx in (2, 1, 3):
            x_copy(kind, dx, d).start()

    def kv_block(kind, d, cc):
        return kv.at[kind, cc * NY + (y + d + NY) % NY]

    def y_gather(kind):
        ref = kv_block(kind, 0, core)
        if NC == 2:
            core_copy(kind, 0).start()
        for d in y_order[1:]:
            remote(ref, ref, kv_send.at[kind, d], kv_recv.at[kind, d], at_y(d)).start()

    def core_copy(kind, d):
        ref = kv_block(kind, d, core)
        return remote(ref, ref, ks_send.at[kind, d], ks_recv.at[kind, d], sibling)

    def y_arrived(kind, d):
        ref = kv_block(kind, d, core)
        back = (NY - d) % NY
        remote(ref, ref, kv_send.at[kind, back], kv_recv.at[kind, back], at_y(1)).wait_recv()
        if NC == 2:
            core_copy(kind, d).start()

    def core_arrived(kind, d):
        ref = kv_block(kind, d, NC - 1 - core)
        remote(ref, ref, ks_send.at[kind, d], ks_recv.at[kind, d], sibling).wait_recv()

    for kind in (0, 2, 1, 3):
        for d in z_order[1:]:
            a_copy(kind, d).start()
    local[2].wait()
    x_piece(0, 0)

    row_in = lax.broadcasted_iota(jnp.int32, (ROWS, HD), 0)
    for cc in range(NC):
        for yy in range(NY):
            for zz in range(NZ):
                base = order[(yy // 2) * (NZ * NC) + zz * NC + cc] * 128 + ((yy % 2) * NX + x) * ROWS
                pos_u[cc * NY + yy, pl.ds(zz * ROWS, ROWS), :] = row_in + base
    t_lane = lax.broadcasted_iota(jnp.int32, (8, T), 1)
    row_pos = jnp.zeros((8, T), jnp.int32)
    for zz in range(NZ):
        base = order[yh * (NZ * NC) + zz * NC + core] * 128 + yl * NX * ROWS
        row_pos = jnp.where(t_lane // ROWS == zz, base + t_lane % ROWS, row_pos)
    pos_t[...] = row_pos

    local[0].wait()
    local[1].wait()
    lane = lax.broadcasted_iota(jnp.int32, (ROWS, HD), 1)

    def rowdots(zz, carry):
        spread = jnp.zeros((ROWS, HD), F32)
        for h in range(GROUP):
            cols = pl.ds(pl.multiple_of(zz * W + h * HD, HD), HD)
            dots = jnp.sum(g_buf[:, cols].astype(F32) * o_buf[:, cols].astype(F32), axis=1, keepdims=True)
            spread = jnp.where(lane // 32 == h, dots, spread)
        high = spread.astype(BF16).astype(F32)
        rest = spread - high
        middle = rest.astype(BF16).astype(F32)
        low = rest - middle
        piece = lane % 32
        pieces = jnp.where(piece == 0, high, jnp.where(piece == 1, middle, jnp.where(piece == 2, low, 0.0)))
        r_buf[zz] = pieces.astype(BF16)
        return carry

    lax.fori_loop(0, NZ, rowdots, 0)
    r_own[zrow(z), :] = r_buf[z]
    for d in z_order[1:]:
        a_copy(4, d).start()
    for copy in local[3:]:
        copy.wait()

    for d in z_order[1:3]:
        x_piece(0, d)
    for d in z_order[1:]:
        a_arrived(0, d)
    y_gather(0)
    for d in z_order[3:]:
        x_piece(0, d)
    for d in z_order[1:]:
        a_arrived(1, d)
    y_gather(1)

    scale = INV_ROOT * LOG2E

    def key_rows(which, j):
        return kv[which, pl.ds(2 * j, 2)].reshape(2 * T, HD)

    def side_by_side(kind, xs):
        return jnp.concatenate([qg[kind, xs, :, h * HD:(h + 1) * HD].T for h in range(GROUP)], axis=1)

    def stacked(kind, xs):
        return jnp.concatenate([qg[kind, xs, :, h * HD:(h + 1) * HD] for h in range(GROUP)], axis=0)

    def score_tile(j, xs):
        s = dot_nn(key_rows(0, j), qt_buf[xs])
        seen = pos_u[pl.ds(2 * j, 2)].reshape(2 * T, HD)[:, :T] <= pos_t[0:1, :] + xs * ROWS
        for h in range(GROUP):
            cols = slice(h * T, (h + 1) * T)
            part = jnp.where(seen, s[:, cols] * scale, NEG)
            top = jnp.max(part, axis=0, keepdims=True)
            e = jnp.exp2(part - top)
            e_buf[j, xs, :, cols] = e
            m_buf[j, xs, :, cols] = top
            l_buf[j, xs, :, cols] = jnp.sum(e, axis=0, keepdims=True)

    def score_chunk(j):
        for xs in range(NX):
            score_tile(j, xs)

    mate = (1 - 2 * yl + NY) % NY
    near_tiles = [(cc, dx) for cc in range(NC) for dx in (0, 1, 3, 2)]
    per_piece = len(near_tiles) // NZ
    for i, d in enumerate(z_order):
        x_piece(1, d)
        for cc, dx in near_tiles[i * per_piece:(i + 1) * per_piece]:
            xs = (x + NX - dx) % NX
            if cc == 0:
                if dx == 0:
                    y_arrived(0, mate)
                else:
                    for dd in z_order:
                        x_arrived(0, dx, dd)
                qt_buf[xs] = side_by_side(0, xs)
            elif dx == 0:
                core_arrived(0, 0)
                core_arrived(0, mate)
            score_tile(((core + cc) % NC) * NP + yh, xs)

    for d in z_order[1:]:
        a_arrived(4, d)
    pick_row = lax.broadcasted_iota(jnp.int32, (8, HD), 0)
    pick_lane = lax.broadcasted_iota(jnp.int32, (8, HD), 1)
    pick = jnp.where((pick_lane // 32 == pick_row) & (pick_lane % 32 < 3), 1.0, 0.0).astype(BF16)
    rd_buf[x] = dot_nt(pick, r_own[...])

    def rd_copy(d):
        return remote(rd_buf.at[x], rd_buf.at[x], rd_send.at[d], rd_recv.at[d], at_x(d))

    for d in range(1, NX):
        rd_copy(d).start()

    def pair_offsets(p):
        return [(2 * p + e - y + 2 * NY) % NY for e in (0, 1)]

    def near_pair(i):
        rel = i + i // 2 - 2 * (i // 3) if NP == 4 else i
        return (yh + rel) % NP

    def scores_of(p, both, from_sibling):
        for d in both:
            y_arrived(0, d)
        score_chunk(core * NP + p)
        if NC == 2:
            for d in from_sibling:
                core_arrived(0, d)
            score_chunk((NC - 1 - core) * NP + p)

    def scores_far(i, carry):
        p = near_pair(i)
        scores_of(p, pair_offsets(p), pair_offsets(p))
        return carry

    lax.fori_loop(1, NP, scores_far, 0)
    for xs in range(NX):
        top = m_buf[0, xs]
        for j in range(1, NJ):
            top = jnp.maximum(top, m_buf[j, xs])
        total = l_buf[0, xs] * jnp.exp2(m_buf[0, xs] - top)
        for j in range(1, NJ):
            total = total + l_buf[j, xs] * jnp.exp2(m_buf[j, xs] - top)
        st[x, xs, 0:1, :] = top
        st[x, xs, 1:2, :] = total

    def st_copy(d):
        return remote(st.at[x], st.at[x], st_send.at[d], st_recv.at[d], at_x(d))

    for d in range(1, NX):
        st_copy(d).start()

    for dx in range(1, NX):
        for d in z_order:
            x_arrived(1, dx, d)
    for xs in range(NX):
        gt_buf[xs] = side_by_side(1, xs)
    for d in range(1, NX):
        ref = rd_buf.at[(x + NX - d) % NX]
        remote(ref, ref, rd_send.at[d], rd_recv.at[d], at_x(d)).wait_recv()
    for b in range(NC * NY):
        kt_buf[:, b * T:(b + 1) * T] = kv[0, b].T

    def dprobs_chunk(j):
        for xs in range(NX):
            rowdot = jnp.concatenate([rd_buf[xs, h:h + 1, :] for h in range(GROUP)], axis=1)
            dp_buf[j, xs] = dot_nn(key_rows(1, j), gt_buf[xs]) - rowdot

    def dprobs_of(p, both, from_sibling):
        for d in both:
            y_arrived(1, d)
        dprobs_chunk(core * NP + p)
        if NC == 2:
            for d in from_sibling:
                core_arrived(1, d)
            dprobs_chunk((NC - 1 - core) * NP + p)

    def dprobs_far(i, carry):
        p = near_pair(i)
        dprobs_of(p, pair_offsets(p), pair_offsets(p))
        return carry

    dprobs_of(yh, [mate], [0, mate])
    lax.fori_loop(1, NP, dprobs_far, 0)
    for d in range(1, NX):
        ref = st.at[(x + NX - d) % NX]
        remote(ref, ref, st_send.at[d], st_recv.at[d], at_x(d)).wait_recv()
    for xs in range(NX):
        top = st[0, xs, 0:1, :]
        for other in range(1, NX):
            top = jnp.maximum(top, st[other, xs, 0:1, :])
        total = jnp.zeros((1, GROUP * T), F32)
        for other in range(NX):
            total = total + st[other, xs, 1:2, :] * jnp.exp2(st[other, xs, 0:1, :] - top)
        lse[xs] = top + jnp.log2(total)

    for j in range(NJ):
        for xs in range(NX):
            m_buf[j, xs] = jnp.exp2(m_buf[j, xs] - lse[xs])

    def sib_copy(kind, p):
        return remote(sib_send.at[kind, p], sib_recv.at[kind, p], sb_send.at[kind, p], sb_recv.at[kind, p], sibling)

    def y_copy(kind, p, half_of):
        d = (2 * p + half_of - y + 2 * NY) % NY
        src = y_send.at[kind, p, pl.ds(pl.multiple_of(half_of * T, T), T), :]
        return remote(src, y_recv.at[kind, d], yd_send.at[kind, d], yd_recv.at[kind, d], at_y(d))

    def key_chunk(j):
        part = jnp.zeros((2 * T, HD), F32)
        for xs in range(NX):
            ds = (e_buf[j, xs] * m_buf[j, xs] * dp_buf[j, xs]).astype(BF16)
            ds_buf[xs, j] = ds
            part = part + dot_nn(ds, stacked(0, xs))
        return part

    def value_chunk(j):
        part = jnp.zeros((2 * T, HD), F32)
        for xs in range(NX):
            part = part + dot_nn((e_buf[j, xs] * m_buf[j, xs]).astype(BF16), stacked(1, xs))
        return part

    def both_cores(kind, chunk, p):
        if NC == 2:
            sib_send[kind, p] = chunk((NC - 1 - core) * NP + p).astype(BF16)
            sib_copy(kind, p).start()
        part = chunk(core * NP + p)
        if NC == 2:
            sib_copy(kind, p).wait_recv()
            part = part + sib_recv[kind, p].astype(F32)
        y_send[kind, p] = part.astype(BF16)
        return part

    def all_pairs(kind, chunk):
        def far_pair(i, carry):
            p = near_pair(NP - 1 - i)
            both_cores(kind, chunk, p)
            y_copy(kind, p, 0).start()
            y_copy(kind, p, 1).start()
            return carry

        lax.fori_loop(0, NP - 1, far_pair, 0)
        own_dkv[kind] = both_cores(kind, chunk, yh)
        y_copy(kind, yh, 1 - yl).start()

    all_pairs(0, key_chunk)

    def dq_copy(d):
        to = (x + d) % NX
        return remote(dq_send.at[to], dq_recv.at[d], xd_send.at[d], xd_recv.at[d], at_x(d))

    def query_block(xs):
        return dot_nn(kt_buf[...], ds_buf[xs].reshape(NJ * 2 * T, GROUP * T))

    for d in (2, 1, 3):
        to = (x + d) % NX
        dq_send[to] = query_block(to).astype(BF16)
        dq_copy(d).start()
    dq_own[...] = query_block(x)

    all_pairs(1, value_chunk)

    def out_copy(kind, d):
        to = (z + d) % NZ
        src, dst = {
            0: (dq_fin.at[zrow(to), :], q_out.at[:, zcol(z, W)]),
            1: (dkv_fin.at[0, zrow(to), :], k_out.at[:, zcol(z, HD)]),
            2: (dkv_fin.at[1, zrow(to), :], v_out.at[:, zcol(z, HD)]),
        }[kind]
        if d == 0:
            return pltpu.make_async_copy(src, dst, zo_send.at[kind, 0])
        return remote(src, dst, zo_send.at[kind, d], zo_recv.at[kind, d], at_z(d))

    own_rows = pl.ds(pl.multiple_of(yl * T, T), T)

    dq = dq_own[...]
    for d in range(1, NX):
        ref = dq_recv.at[d]
        remote(ref, ref, xd_send.at[d], xd_recv.at[d], at_x(d)).wait_recv()
        dq = dq + dq_recv[d].astype(F32)
    dq = dq * INV_ROOT
    for h in range(GROUP):
        dq_fin[:, h * HD:(h + 1) * HD] = dq[:, h * T:(h + 1) * T].T.astype(BF16)
    for d in z_order:
        out_copy(0, d).start()
    for kind, factor in ((0, INV_ROOT), (1, 1.0)):
        total = own_dkv[kind, own_rows, :]
        for d in range(1, NY):
            ref = y_recv.at[kind, d]
            remote(ref, ref, yd_send.at[kind, d], yd_recv.at[kind, d], at_y(d)).wait_recv()
            total = total + y_recv[kind, d].astype(F32)
        dkv_fin[kind] = (total * factor).astype(BF16)
        for d in z_order:
            out_copy(1 + kind, d).start()

    for kind in range(3):
        out_copy(kind, 0).wait()
    for d in z_order[1:]:
        src = (z + NZ - d) % NZ
        for kind, ref in (
            (0, q_out.at[:, zcol(src, W)]),
            (1, k_out.at[:, zcol(src, HD)]),
            (2, v_out.at[:, zcol(src, HD)]),
        ):
            remote(ref, ref, zo_send.at[kind, d], zo_recv.at[kind, d], at_z(d)).wait_recv()
    for d in z_order[1:]:
        for kind in range(5):
            a_copy(kind, d).wait_send()
        for kind in range(3):
            out_copy(kind, d).wait_send()
    for d in range(NZ):
        for dx in range(1, NX):
            x_copy(0, dx, d).wait_send()
            x_copy(1, dx, d).wait_send()
    for kind in (0, 1):
        ref = kv_block(kind, 0, core)
        for d in range(1, NY):
            remote(ref, ref, kv_send.at[kind, d], kv_recv.at[kind, d], at_y(d)).wait_send()
        if NC == 2:
            for d in range(NY):
                core_copy(kind, d).wait_send()
    if NC == 2:
        for p in range(NP):
            sib_copy(0, p).wait_send()
            sib_copy(1, p).wait_send()
    for d in range(1, NX):
        rd_copy(d).wait_send()
        st_copy(d).wait_send()
        dq_copy(d).wait_send()
    for d in range(1, NY):
        for kind in (0, 1):
            ref = y_recv.at[kind, d]
            remote(ref, ref, yd_send.at[kind, d], yd_recv.at[kind, d], at_y(d)).wait_send()


def copy_kernel(q_from, k_from, v_from, q_to, k_to, v_to, sem):
    copies = [
        pltpu.make_async_copy(q_from, q_to, sem.at[0]),
        pltpu.make_async_copy(k_from, k_to, sem.at[1]),
        pltpu.make_async_copy(v_from, v_to, sem.at[2]),
    ]
    for copy in copies:
        copy.start()
    for copy in copies:
        copy.wait()


def on_device(queries, keys, values, outputs, grad_out, span_order):
    T = NZ * ROWS
    NJ = NC * NY // 2
    NP = NY // 2
    vmem = pltpu.VMEM
    dma = pltpu.SemaphoreType.DMA
    width = W * NZ
    kv_width = HD * NZ
    scratch = [
        vmem((ROWS, width), BF16),
        vmem((ROWS, width), BF16),
        vmem((NZ, ROWS, HD), BF16),
        vmem((T, HD), BF16),
        vmem((NX, 8, T), F32),
        vmem((2, NX, T, W), BF16),
        vmem((2, NC * NY, T, HD), BF16),
        vmem((NC * NY, T, HD), jnp.int32),
        vmem((8, T), jnp.int32),
        vmem((NX, HD, GROUP * T), BF16),
        vmem((NX, HD, GROUP * T), BF16),
        vmem((HD, NC * NY * T), BF16),
        vmem((NJ, NX, 2 * T, GROUP * T), F32),
        vmem((NJ, NX, 2 * T, GROUP * T), F32),
        vmem((NX, NJ, 2 * T, GROUP * T), BF16),
        vmem((NJ, NX, 1, GROUP * T), F32),
        vmem((NJ, NX, 1, GROUP * T), F32),
        vmem((NX, NX, 2, GROUP * T), F32),
        vmem((NX, 1, GROUP * T), F32),
        vmem((HD, GROUP * T), F32),
        vmem((NX, HD, GROUP * T), BF16),
        vmem((NX, HD, GROUP * T), BF16),
        vmem((2, NP, 2 * T, HD), BF16),
        vmem((2, NP, 2 * T, HD), BF16),
        vmem((2, NP, 2 * T, HD), BF16),
        vmem((2, NY, T, HD), BF16),
        vmem((2, 2 * T, HD), F32),
        vmem((T, W), BF16),
        vmem((2, T, HD), BF16),
        dma((6,)),
        dma((5, NZ)), dma((5, NZ)),
        dma((2, NX, NZ)), dma((2, NX, NZ)),
        dma((NX,)), dma((NX,)),
        dma((2, NY)), dma((2, NY)),
        dma((2, NY)), dma((2, NY)),
        dma((NX,)), dma((NX,)),
        dma((2, NP)), dma((2, NP)),
        dma((2, NY)), dma((2, NY)),
        dma((NX,)), dma((NX,)),
        dma((3, NZ)), dma((3, NZ)),
    ]
    anywhere = pl.BlockSpec(memory_space=pl.ANY)
    in_vmem = pl.BlockSpec(memory_space=pltpu.VMEM)
    shapes = (
        jax.ShapeDtypeStruct((ROWS, width), BF16),
        jax.ShapeDtypeStruct((ROWS, kv_width), BF16),
        jax.ShapeDtypeStruct((ROWS, kv_width), BF16),
    )
    grads = pl.pallas_call(
        kernel,
        out_shape=shapes,
        in_specs=[anywhere] * 5 + [pl.BlockSpec(memory_space=pltpu.SMEM)],
        out_specs=(in_vmem, in_vmem, in_vmem),
        scratch_shapes=scratch,
        compiler_params=pltpu.CompilerParams(
            collective_id=0, has_side_effects=True, vmem_limit_bytes=56 * 1024 * 1024
        ),
    )(queries, keys, values, outputs, grad_out, span_order)
    return pl.pallas_call(
        copy_kernel,
        out_shape=shapes,
        in_specs=[in_vmem, in_vmem, in_vmem],
        out_specs=(anywhere, anywhere, anywhere),
        scratch_shapes=[dma((3,))],
    )(*grads)


def solution(mesh):
    rows = P(("blk", "head"), None)
    return jax.shard_map(
        on_device,
        mesh=mesh,
        in_specs=(rows, rows, rows, rows, rows, P()),
        out_specs=(rows, rows, rows),
        check_vma=False,
    )
```

time: 91.2 us -> 71 us (0.78)
  Pallas kernels: 87.4 us -> 70.1 us
  local copies, waits for them, and re-layouts: 2.96 us -> 0 us
    pallas_call x1 -> x2, Pallas kernels: 87.4 us -> 70.1 us  [the longest x1 68.5 us: on_device(): pl.pallas_call(kernel, out_shape=shapes, in_specs=[anywhere] * 5 + [pl.Bl...]
    unnamed x7 -> x0, local copies, waits for them, and re-layouts: 2.96 us -> none
where the time goes in v2:
time: 71 us; the launch traced here: 70.8 us
  Pallas kernels  70.1 us (99%)
    pallas_call x1, Pallas kernels, on_device(): pl.pallas_call(kernel, out_shape=shapes, in_specs=[anywhere] * 5 + [pl.Bl...  68.5 us
    pallas_call x1, Pallas kernels, on_device(): pl.pallas_call(copy_kernel, out_shape=shapes, in_specs=[in_vmem, in_vmem,...  1.62 us

profile of v2, /device:TPU:1, one launch (start us, length us, event | category | flops | bytes accessed | tf_op | source)
XLA Modules:
  0.0 70.8 jit_solution(7703827245299103362)
XLA Ops:
  0.6 68.5 %shard_map.85 = (bf16[16,4096]{1,0:T(8,128)(2,1)}, bf16[16,1024]{1,0:T(8,128)(2,1)}, bf16[16,1024]{1,0:T(8,128)(2,1)}) custom-call(bf16[16,4096]{1,0:T(8,128)(2,1)} %q_in.1, bf16[16,1024]{1,0:T(8,128)(2,1)} %k_in.1, bf16[16,1024]{1,0:T(8,128)(2,1)} %v_in.1, bf16[16,4096]{1,0:T(8,128)(2,1)} %o_in.1, bf16[16,4096]{1,0:T(8,128)(2,1)} %g_in.1, s32[64]{0:T(128)} %order.1), custom_call_target="tpu_custom_call" | custom-call | tf_op jit(solution)/shard_map/pallas_call | solution.py:581
  69.2 1.6 %shard_map.86 = (bf16[16,4096]{1,0:T(8,128)(2,1)}, bf16[16,1024]{1,0:T(8,128)(2,1)}, bf16[16,1024]{1,0:T(8,128)(2,1)}) custom-call(bf16[16,4096]{1,0:T(8,128)(2,1)} %get-tuple-element.6.q_from, bf16[16,1024]{1,0:T(8,128)(2,1)} %get-tuple-element.7.k_from, bf16[16,1024]{1,0:T(8,128)(2,1)} %get-tuple-element.8.v_from), custom_call_target="tpu_custom_call" | custom-call | tf_op jit(solution)/shard_map/pallas_call | solution.py:591

commit v3 on v2

--- a/solution.py
+++ b/solution.py
@@ -48,7 +48,7 @@
     o_buf, g_buf, r_buf, r_own, rd_buf, qg, kv, pos_u, pos_t, qt_buf, gt_buf, kt_buf, e_buf, dp_buf, ds_buf, m_buf, l_buf, st, lse,
     dq_own, dq_send, dq_recv, sib_send, sib_recv, y_send, y_recv, own_dkv, dq_fin, dkv_fin,
     loc_sem, a_send, a_recv, x_send, x_recv, rd_send, rd_recv, kv_send, kv_recv,
-    ks_send, ks_recv, st_send, st_recv, sb_send, sb_recv, yd_send, yd_recv, xd_send, xd_recv, zo_send, zo_recv,
+    ks_send, ks_recv, st_send, st_recv, sb_send, sb_recv, yd_send, yd_recv, xd_send, xd_recv, zo_send, zo_recv, zl_sem,
 ):
     T = NZ * ROWS
     NJ = NC * NY // 2
@@ -121,7 +121,7 @@
             3: (g_in.at[:, zcol(to, W)], qg.at[1, x, zrow(z), :]),
             4: (r_buf.at[to], r_own.at[zrow(z), :]),
         }[kind]
-        return remote(src, dst, a_send.at[kind, d], a_recv.at[kind, d], at_z(d))
+        return remote(src, dst, a_send.at[kind], a_recv.at[kind, d], at_z(d))
 
     def a_arrived(kind, d):
         row = zrow((z + NZ - d) % NZ)
@@ -132,15 +132,15 @@
             3: qg.at[1, x, row, :],
             4: r_own.at[row, :],
         }[kind]
-        remote(ref, ref, a_send.at[kind, d], a_recv.at[kind, d], at_z(d)).wait_recv()
+        remote(ref, ref, a_send.at[kind], a_recv.at[kind, d], at_z(d)).wait_recv()
 
     def x_copy(kind, dx, d):
         ref = qg.at[kind, x, zrow((z + NZ - d) % NZ), :]
-        return remote(ref, ref, x_send.at[kind, dx, d], x_recv.at[kind, dx, d], at_x(dx))
-
-    def x_arrived(kind, dx, d):
-        ref = qg.at[kind, (x + NX - dx) % NX, zrow((z + NZ - d) % NZ), :]
-        remote(ref, ref, x_send.at[kind, dx, d], x_recv.at[kind, dx, d], at_x(dx)).wait_recv()
+        return remote(ref, ref, x_send.at[kind, dx], x_recv.at[kind, dx], at_x(dx))
+
+    def x_whole(kind, dx):
+        ref = qg.at[kind, (x + NX - dx) % NX]
+        return remote(ref, ref, x_send.at[kind, dx], x_recv.at[kind, dx], at_x(dx))
 
     def x_piece(kind, d):
         if d > 0:
@@ -267,8 +267,7 @@
                 if dx == 0:
                     y_arrived(0, mate)
                 else:
-                    for dd in z_order:
-                        x_arrived(0, dx, dd)
+                    x_whole(0, dx).wait_recv()
                 qt_buf[xs] = side_by_side(0, xs)
             elif dx == 0:
                 core_arrived(0, 0)
@@ -295,21 +294,31 @@
         rel = i + i // 2 - 2 * (i // 3) if NP == 4 else i
         return (yh + rel) % NP
 
-    def scores_of(p, both, from_sibling):
-        for d in both:
-            y_arrived(0, d)
-        score_chunk(core * NP + p)
+    def own_blocks(kind, chunk, i):
+        p = near_pair(i)
+        for d in pair_offsets(p):
+            y_arrived(kind, d)
+        chunk(core * NP + p)
+
+    def other_blocks(kind, chunk, i):
         if NC == 2:
-            for d in from_sibling:
-                core_arrived(0, d)
-            score_chunk((NC - 1 - core) * NP + p)
-
-    def scores_far(i, carry):
-        p = near_pair(i)
-        scores_of(p, pair_offsets(p), pair_offsets(p))
-        return carry
-
-    lax.fori_loop(1, NP, scores_far, 0)
+            p = near_pair(i)
+            for d in pair_offsets(p):
+                core_arrived(kind, d)
+            chunk((NC - 1 - core) * NP + p)
+
+    def skewed(kind, chunk):
+        def body(i, carry):
+            own_blocks(kind, chunk, i)
+            other_blocks(kind, chunk, i - 1)
+            return carry
+
+        return body
+
+    if NP > 1:
+        own_blocks(0, score_chunk, 1)
+        lax.fori_loop(2, NP, skewed(0, score_chunk), 0)
+        other_blocks(0, score_chunk, NP - 1)
     for xs in range(NX):
         top = m_buf[0, xs]
         for j in range(1, NJ):
@@ -327,8 +336,7 @@
         st_copy(d).start()
 
     for dx in range(1, NX):
-        for d in z_order:
-            x_arrived(1, dx, d)
+        x_whole(1, dx).wait_recv()
     for xs in range(NX):
         gt_buf[xs] = side_by_side(1, xs)
     for d in range(1, NX):
@@ -342,22 +350,10 @@
             rowdot = jnp.concatenate([rd_buf[xs, h:h + 1, :] for h in range(GROUP)], axis=1)
             dp_buf[j, xs] = dot_nn(key_rows(1, j), gt_buf[xs]) - rowdot
 
-    def dprobs_of(p, both, from_sibling):
-        for d in both:
-            y_arrived(1, d)
-        dprobs_chunk(core * NP + p)
-        if NC == 2:
-            for d in from_sibling:
-                core_arrived(1, d)
-            dprobs_chunk((NC - 1 - core) * NP + p)
-
-    def dprobs_far(i, carry):
-        p = near_pair(i)
-        dprobs_of(p, pair_offsets(p), pair_offsets(p))
-        return carry
-
-    dprobs_of(yh, [mate], [0, mate])
-    lax.fori_loop(1, NP, dprobs_far, 0)
+    y_arrived(1, mate)
+    dprobs_chunk(core * NP + yh)
+    lax.fori_loop(1, NP, skewed(1, dprobs_chunk), 0)
+    other_blocks(1, dprobs_chunk, NP - 1)
     for d in range(1, NX):
         ref = st.at[(x + NX - d) % NX]
         remote(ref, ref, st_send.at[d], st_recv.at[d], at_x(d)).wait_recv()
@@ -396,27 +392,32 @@
             part = part + dot_nn((e_buf[j, xs] * m_buf[j, xs]).astype(BF16), stacked(1, xs))
         return part
 
-    def both_cores(kind, chunk, p):
-        if NC == 2:
+    def all_pairs(kind, chunk):
+        def for_sibling(i, carry):
+            p = near_pair(NP - 1 - i)
             sib_send[kind, p] = chunk((NC - 1 - core) * NP + p).astype(BF16)
             sib_copy(kind, p).start()
-        part = chunk(core * NP + p)
-        if NC == 2:
-            sib_copy(kind, p).wait_recv()
-            part = part + sib_recv[kind, p].astype(F32)
-        y_send[kind, p] = part.astype(BF16)
-        return part
-
-    def all_pairs(kind, chunk):
+            return carry
+
+        def own_pair(p):
+            part = chunk(core * NP + p)
+            if NC == 2:
+                sib_copy(kind, p).wait_recv()
+                part = part + sib_recv[kind, p].astype(F32)
+            y_send[kind, p] = part.astype(BF16)
+            return part
+
         def far_pair(i, carry):
             p = near_pair(NP - 1 - i)
-            both_cores(kind, chunk, p)
+            own_pair(p)
             y_copy(kind, p, 0).start()
             y_copy(kind, p, 1).start()
             return carry
 
+        if NC == 2:
+            lax.fori_loop(0, NP, for_sibling, 0)
         lax.fori_loop(0, NP - 1, far_pair, 0)
-        own_dkv[kind] = both_cores(kind, chunk, yh)
+        own_dkv[kind] = own_pair(yh)
         y_copy(kind, yh, 1 - yl).start()
 
     all_pairs(0, key_chunk)
@@ -435,6 +436,31 @@
     dq_own[...] = query_block(x)
 
     all_pairs(1, value_chunk)
+
+    if NZ > 1:
+        for kind, ref in enumerate((
+            k_in.at[:, pl.ds(0, (NZ - 1) * HD)],
+            v_in.at[:, pl.ds(0, (NZ - 1) * HD)],
+            q_in.at[:, pl.ds(0, (NZ - 1) * W)],
+            g_in.at[:, pl.ds(0, (NZ - 1) * W)],
+            r_buf.at[pl.ds(0, NZ - 1)],
+        )):
+            remote(ref, ref, a_send.at[kind], a_recv.at[kind, 1], at_z(1)).wait_send()
+    for kind in (0, 1):
+        for dx in range(1, NX):
+            x_whole(kind, dx).wait_send()
+        ref = kv_block(kind, 0, core)
+        for d in range(1, NY):
+            remote(ref, ref, kv_send.at[kind, d], kv_recv.at[kind, d], at_y(d)).wait_send()
+        if NC == 2:
+            for d in range(NY):
+                core_copy(kind, d).wait_send()
+            for p in range(NP):
+                sib_copy(kind, p).wait_send()
+    for d in range(1, NX):
+        rd_copy(d).wait_send()
+        st_copy(d).wait_send()
+        dq_copy(d).wait_send()
 
     def out_copy(kind, d):
         to = (z + d) % NZ
@@ -444,8 +470,12 @@
             2: (dkv_fin.at[1, zrow(to), :], v_out.at[:, zcol(z, HD)]),
         }[kind]
         if d == 0:
-            return pltpu.make_async_copy(src, dst, zo_send.at[kind, 0])
-        return remote(src, dst, zo_send.at[kind, d], zo_recv.at[kind, d], at_z(d))
+            return pltpu.make_async_copy(src, dst, zl_sem.at[kind])
+        return remote(src, dst, zo_send.at[kind], zo_recv.at[kind], at_z(d))
+
+    def out_whole(kind):
+        ref = (q_out.at[:, pl.ds(0, (NZ - 1) * W)], k_out.at[:, pl.ds(0, (NZ - 1) * HD)], v_out.at[:, pl.ds(0, (NZ - 1) * HD)])[kind]
+        return remote(ref, ref, zo_send.at[kind], zo_recv.at[kind], at_z(1))
 
     own_rows = pl.ds(pl.multiple_of(yl * T, T), T)
 
@@ -469,44 +499,14 @@
         for d in z_order:
             out_copy(1 + kind, d).start()
 
-    for kind in range(3):
-        out_copy(kind, 0).wait()
-    for d in z_order[1:]:
-        src = (z + NZ - d) % NZ
-        for kind, ref in (
-            (0, q_out.at[:, zcol(src, W)]),
-            (1, k_out.at[:, zcol(src, HD)]),
-            (2, v_out.at[:, zcol(src, HD)]),
-        ):
-            remote(ref, ref, zo_send.at[kind, d], zo_recv.at[kind, d], at_z(d)).wait_recv()
-    for d in z_order[1:]:
-        for kind in range(5):
-            a_copy(kind, d).wait_send()
-        for kind in range(3):
-            out_copy(kind, d).wait_send()
-    for d in range(NZ):
-        for dx in range(1, NX):
-            x_copy(0, dx, d).wait_send()
-            x_copy(1, dx, d).wait_send()
-    for kind in (0, 1):
-        ref = kv_block(kind, 0, core)
-        for d in range(1, NY):
-            remote(ref, ref, kv_send.at[kind, d], kv_recv.at[kind, d], at_y(d)).wait_send()
-        if NC == 2:
-            for d in range(NY):
-                core_copy(kind, d).wait_send()
-    if NC == 2:
-        for p in range(NP):
-            sib_copy(0, p).wait_send()
-            sib_copy(1, p).wait_send()
-    for d in range(1, NX):
-        rd_copy(d).wait_send()
-        st_copy(d).wait_send()
-        dq_copy(d).wait_send()
     for d in range(1, NY):
         for kind in (0, 1):
             ref = y_recv.at[kind, d]
             remote(ref, ref, yd_send.at[kind, d], yd_recv.at[kind, d], at_y(d)).wait_send()
+    for kind in range(3):
+        out_copy(kind, 0).wait()
+        if NZ > 1:
+            out_whole(kind).wait()
 
 
 def copy_kernel(q_from, k_from, v_from, q_to, k_to, v_to, sem):
@@ -560,8 +560,8 @@
         vmem((T, W), BF16),
         vmem((2, T, HD), BF16),
         dma((6,)),
-        dma((5, NZ)), dma((5, NZ)),
-        dma((2, NX, NZ)), dma((2, NX, NZ)),
+        dma((5,)), dma((5, NZ)),
+        dma((2, NX)), dma((2, NX)),
         dma((NX,)), dma((NX,)),
         dma((2, NY)), dma((2, NY)),
         dma((2, NY)), dma((2, NY)),
@@ -569,7 +569,7 @@
         dma((2, NP)), dma((2, NP)),
         dma((2, NY)), dma((2, NY)),
         dma((NX,)), dma((NX,)),
-        dma((3, NZ)), dma((3, NZ)),
+        dma((3,)), dma((3,)), dma((3,)),
     ]
     anywhere = pl.BlockSpec(memory_space=pl.ANY)
     in_vmem = pl.BlockSpec(memory_space=pltpu.VMEM)

time: 71 us -> 64.6 us (0.910)
  Pallas kernels: 70.1 us -> 63.2 us
    pallas_call x1, Pallas kernels: 68.5 us -> 61.6 us  [on_device(): pl.pallas_call(kernel, out_shape=shapes, in_specs=[anywhere] * 5 + [pl.Bl...]
where the time goes in v3:
time: 64.6 us; the launch traced here: 63.9 us
  Pallas kernels  63.2 us (98%)
    pallas_call x1, Pallas kernels, on_device(): pl.pallas_call(kernel, out_shape=shapes, in_specs=[anywhere] * 5 + [pl.Bl...  61.6 us
    pallas_call x1, Pallas kernels, on_device(): pl.pallas_call(copy_kernel, out_shape=shapes, in_specs=[in_vmem, in_vmem,...  1.62 us

profile of v3, /device:TPU:1, one launch (start us, length us, event | category | flops | bytes accessed | tf_op | source)
XLA Modules:
  0.0 63.9 jit_solution(17542192743507889294)
XLA Ops:
  0.6 61.6 %shard_map.85 = (bf16[16,4096]{1,0:T(8,128)(2,1)}, bf16[16,1024]{1,0:T(8,128)(2,1)}, bf16[16,1024]{1,0:T(8,128)(2,1)}) custom-call(bf16[16,4096]{1,0:T(8,128)(2,1)} %q_in.1, bf16[16,1024]{1,0:T(8,128)(2,1)} %k_in.1, bf16[16,1024]{1,0:T(8,128)(2,1)} %v_in.1, bf16[16,4096]{1,0:T(8,128)(2,1)} %o_in.1, bf16[16,4096]{1,0:T(8,128)(2,1)} %g_in.1, s32[64]{0:T(128)} %order.1), custom_call_target="tpu_custom_call" | custom-call | tf_op jit(solution)/shard_map/pallas_call | solution.py:581
  62.2 1.6 %shard_map.86 = (bf16[16,4096]{1,0:T(8,128)(2,1)}, bf16[16,1024]{1,0:T(8,128)(2,1)}, bf16[16,1024]{1,0:T(8,128)(2,1)}) custom-call(bf16[16,4096]{1,0:T(8,128)(2,1)} %get-tuple-element.6.q_from, bf16[16,1024]{1,0:T(8,128)(2,1)} %get-tuple-element.7.k_from, bf16[16,1024]{1,0:T(8,128)(2,1)} %get-tuple-element.8.v_from), custom_call_target="tpu_custom_call" | custom-call | tf_op jit(solution)/shard_map/pallas_call | solution.py:591

commit v4 on v3

--- a/solution.py
+++ b/solution.py
@@ -111,6 +111,7 @@
 
     z_order = near_first(NZ)
     y_order = near_first(NY)
+    mate = (1 - 2 * yl + NY) % NY
 
     def a_copy(kind, d):
         to = (z + d) % NZ
@@ -155,7 +156,7 @@
         ref = kv_block(kind, 0, core)
         if NC == 2:
             core_copy(kind, 0).start()
-        for d in y_order[1:]:
+        for d in [mate] + y_order[:2:-1] + [NY - mate]:
             remote(ref, ref, kv_send.at[kind, d], kv_recv.at[kind, d], at_y(d)).start()
 
     def core_copy(kind, d):
@@ -256,7 +257,6 @@
         for xs in range(NX):
             score_tile(j, xs)
 
-    mate = (1 - 2 * yl + NY) % NY
     near_tiles = [(cc, dx) for cc in range(NC) for dx in (0, 1, 3, 2)]
     per_piece = len(near_tiles) // NZ
     for i, d in enumerate(z_order):

time: 64.6 us -> 64.7 us (level)
  no operation moved by 1% of the time
where the time goes in v4:
time: 64.7 us; the launch traced here: 64.2 us
  Pallas kernels  63.5 us (98%)
    pallas_call x1, Pallas kernels, on_device(): pl.pallas_call(kernel, out_shape=shapes, in_specs=[anywhere] * 5 + [pl.Bl...  61.9 us
    pallas_call x1, Pallas kernels, on_device(): pl.pallas_call(copy_kernel, out_shape=shapes, in_specs=[in_vmem, in_vmem,...  1.62 us

profile of v4, /device:TPU:1, one launch (start us, length us, event | category | flops | bytes accessed | tf_op | source)
XLA Modules:
  0.0 64.2 jit_solution(2178141651449922764)
XLA Ops:
  0.6 61.9 %shard_map.85 = (bf16[16,4096]{1,0:T(8,128)(2,1)}, bf16[16,1024]{1,0:T(8,128)(2,1)}, bf16[16,1024]{1,0:T(8,128)(2,1)}) custom-call(bf16[16,4096]{1,0:T(8,128)(2,1)} %q_in.1, bf16[16,1024]{1,0:T(8,128)(2,1)} %k_in.1, bf16[16,1024]{1,0:T(8,128)(2,1)} %v_in.1, bf16[16,4096]{1,0:T(8,128)(2,1)} %o_in.1, bf16[16,4096]{1,0:T(8,128)(2,1)} %g_in.1, s32[64]{0:T(128)} %order.1), custom_call_target="tpu_custom_call" | custom-call | tf_op jit(solution)/shard_map/pallas_call | solution.py:581
  62.6 1.6 %shard_map.86 = (bf16[16,4096]{1,0:T(8,128)(2,1)}, bf16[16,1024]{1,0:T(8,128)(2,1)}, bf16[16,1024]{1,0:T(8,128)(2,1)}) custom-call(bf16[16,4096]{1,0:T(8,128)(2,1)} %get-tuple-element.6.q_from, bf16[16,1024]{1,0:T(8,128)(2,1)} %get-tuple-element.7.k_from, bf16[16,1024]{1,0:T(8,128)(2,1)} %get-tuple-element.8.v_from), custom_call_target="tpu_custom_call" | custom-call | tf_op jit(solution)/shard_map/pallas_call | solution.py:591
